TPU v7x, 32 devices: a whole 2x2x4 slice. The times are simulated.
32 devices in a mesh: dp: 16 (over z, x, core), mp: 2 (over y).
Axes of the slice: x: 2, y: 2, z: 4, core: 2. Of those that a mesh axis runs over, the one named last changes fastest.
Arguments:
- tokens: bfloat16 [16, 8, 197, 768], P('dp'), may hold values from -6 to 6
- captions: bfloat16 [16, 512], P('dp'), may hold values from -0.29882812 to 0.29882812
- clip_groups: int32 [16], P('dp'), may hold values from 0 to 3, as said below
- caption_groups: int32 [16], P('dp'), may hold values from 0 to 3, as said below
- msg_weight: bfloat16 [768, 768], replicated, may hold values from -0.21875 to 0.21875
- msg_gain: float32 [768], replicated, may hold values from 0.5 to 1.5
- msg_in: bfloat16 [3, 768, 768], P(None, None, 'mp'), may hold values from -0.21875 to 0.21875
- msg_out: bfloat16 [768, 768], P('mp'), may hold values from -0.625 to 0.625
- frame_gain: float32 [768], replicated, may hold values from 0.5 to 1.5
- frame_in: bfloat16 [3, 768, 768], P(None, None, 'mp'), may hold values from -0.21875 to 0.21875
- frame_out: bfloat16 [768, 768], P('mp'), may hold values from -0.875 to 0.875
- mlp_gain: float32 [768], replicated, may hold values from 0.5 to 1.5
- up_weight: bfloat16 [768, 3072], P(None, 'mp'), may hold values from -0.21875 to 0.21875
- down_weight: bfloat16 [3072, 768], P('mp'), may hold values from -0.15625 to 0.15625
- proj_weight: bfloat16 [768, 512], replicated, may hold values from -0.21875 to 0.21875
- out_cot: bfloat16 [16, 8, 197, 768], P('dp'), may hold values from -6 to 6
Outputs:
- layer_out: bfloat16 [16, 8, 197, 768], P('dp')
- loss: float32 [], replicated
- token_grad: bfloat16 [16, 8, 197, 768], P('dp')
- caption_grad: float32 [16, 512], P('dp')
- msg_weight_grad: float32 [768, 768], P('dp')
- msg_gain_grad: float32 [768], P('dp')
- msg_in_grad: float32 [3, 768, 768], P(None, 'dp', 'mp')
- msg_out_grad: float32 [768, 768], P('mp', 'dp')
- frame_gain_grad: float32 [768], P('dp')
- frame_in_grad: float32 [3, 768, 768], P(None, 'dp', 'mp')
- frame_out_grad: float32 [768, 768], P('mp', 'dp')
- mlp_gain_grad: float32 [768], P('dp')
- up_grad: float32 [768, 3072], P('dp', 'mp')
- down_grad: float32 [3072, 768], P('mp', 'dp')
- proj_grad: float32 [768, 512], P('dp')
Inputs may be any that keep to these rules, and one draw needn't show every extreme that they name: `clip_groups`: each video id is held by exactly 4 clips. `caption_groups`: each video id is held by exactly 4 captions.
All inputs are finite; a program needn't handle non-finite values.
Results may differ from a plain program's by a relative error of at most 0.025.
Values may be sent and summed in bfloat16 or wider, within the bound.
No kernel may reach another device: no remote copies, remote signals or barrier semaphores. Data moves between devices by JAX's collectives and lax.ppermute only.
A program may use at most 192 MiB of HBM per device.

v0:
```python
import jax
import jax.numpy as jnp
from jax import lax
from jax.sharding import PartitionSpec as P

HEADS = 12


softmax_sharpness_factor = 50.0
lowest = -1e30


def shifted(value, axis, by):
    size = lax.axis_size(axis)
    return lax.ppermute(value, axis, [(i, (i + by) % size) for i in range(size)])


def head_total(part):
    share = lax.psum_scatter(part, "mp", scatter_dimension=0, tiled=True)
    return lax.all_gather(share, "mp", axis=0, tiled=True)


def norm_forward(value, gain):
    centered = value - jnp.mean(value, axis=-1, keepdims=True)
    rstd = lax.rsqrt(jnp.mean(centered * centered, axis=-1, keepdims=True) + 1e-05)
    normal = centered * rstd
    return ((normal * gain).astype(jnp.bfloat16), normal, rstd)


def norm_backward(grad, gain, normal, rstd):
    scaled = grad * gain
    inner = (
        scaled
        - jnp.mean(scaled, axis=-1, keepdims=True)
        - normal * jnp.mean(scaled * normal, axis=-1, keepdims=True)
    )
    gain_grad = jnp.sum((grad * normal).reshape(-1, grad.shape[-1]), axis=0)
    return (rstd * inner, gain_grad)


def attn_forward(normed, w_in, w_out):
    batch, length, width = normed.shape
    head_size = width // HEADS
    local = w_in.shape[2]
    packed = jnp.einsum("bsd,kde->kbse", normed, w_in, preferred_element_type=jnp.float32).astype(
        jnp.bfloat16
    )
    shape = (batch, length, local // head_size, head_size)
    query = packed[0].reshape(shape)
    keys = packed[1].reshape(shape)
    values = packed[2].reshape(shape)
    scores = jnp.einsum(
        "bqhe,bkhe->bhqk", query, keys, preferred_element_type=jnp.float32
    ) * head_size ** (-0.5)
    top = jnp.max(scores, axis=-1, keepdims=True)
    logsum = top + jnp.log(jnp.sum(jnp.exp(scores - top), axis=-1, keepdims=True))
    weights = jnp.exp(scores - logsum).astype(jnp.bfloat16)
    context = jnp.einsum("bhqk,bkhe->bqhe", weights, values, preferred_element_type=jnp.float32)
    context = context.reshape(batch, length, local).astype(jnp.bfloat16)
    branch_part = jnp.einsum("bse,ed->bsd", context, w_out, preferred_element_type=jnp.float32)
    return (branch_part, (query, keys, values, logsum, context))


def attn_backward(normed, w_in, w_out, kept, grad_low):
    query, keys, values, logsum, context = kept
    batch, length, heads, head_size = query.shape
    scale = head_size ** (-0.5)
    out_grad = jnp.einsum("bse,bsd->ed", context, grad_low, preferred_element_type=jnp.float32)
    context_grad = jnp.einsum("bsd,ed->bse", grad_low, w_out, preferred_element_type=jnp.float32)
    context_grad = context_grad.astype(jnp.bfloat16).reshape(batch, length, heads, head_size)
    scores = jnp.einsum("bqhe,bkhe->bhqk", query, keys, preferred_element_type=jnp.float32) * scale
    weights = jnp.exp(scores - logsum)
    weight_grad = jnp.einsum(
        "bqhe,bkhe->bhqk", context_grad, values, preferred_element_type=jnp.float32
    )
    value_grad = jnp.einsum(
        "bhqk,bqhe->bkhe",
        weights.astype(jnp.bfloat16),
        context_grad,
        preferred_element_type=jnp.float32,
    )
    score_grad = (
        weights * (weight_grad - jnp.sum(weights * weight_grad, axis=-1, keepdims=True))
    ).astype(jnp.bfloat16)
    query_grad = (
        jnp.einsum("bhqk,bkhe->bqhe", score_grad, keys, preferred_element_type=jnp.float32) * scale
    )
    key_grad = (
        jnp.einsum("bhqk,bqhe->bkhe", score_grad, query, preferred_element_type=jnp.float32) * scale
    )
    stacked = (
        jnp.stack([query_grad, key_grad, value_grad])
        .reshape(3, batch, length, heads * head_size)
        .astype(jnp.bfloat16)
    )
    in_grad = jnp.einsum("bsd,kbse->kde", normed, stacked, preferred_element_type=jnp.float32)
    normed_part = jnp.einsum("kbse,kde->bsd", stacked, w_in, preferred_element_type=jnp.float32)
    return (normed_part, in_grad, out_grad)


def combine(first, second):
    top = jnp.maximum(first[0], second[0])
    total = first[1] * jnp.exp(first[0] - top) + second[1] * jnp.exp(second[0] - top)
    pos_top = jnp.maximum(first[2], second[2])
    pos_total = first[3] * jnp.exp(first[2] - pos_top) + second[3] * jnp.exp(second[2] - pos_top)
    return (top, total, pos_top, pos_total)


def block_stats(scores, positive, axis):
    top = jnp.max(scores, axis=axis)
    total = jnp.sum(jnp.exp(scores - jnp.expand_dims(top, axis)), axis=axis)
    masked = jnp.where(positive, scores, lowest)
    pos_top = jnp.max(masked, axis=axis)
    pos_total = jnp.sum(
        jnp.where(positive, jnp.exp(masked - jnp.expand_dims(pos_top, axis)), 0.0), axis=axis
    )
    return (top, total, pos_top, pos_total)


def score_grads(scores, positive, row_lse, row_plse, column_lse, column_plse):
    dscore = jnp.exp(scores - row_lse[:, None]) - jnp.where(
        positive, jnp.exp(scores - row_plse[:, None]), 0.0
    )
    dscore = (
        dscore
        + jnp.exp(scores - column_lse[None, :])
        - jnp.where(positive, jnp.exp(scores - column_plse[None, :]), 0.0)
    )
    return (0.5 * dscore).astype(jnp.bfloat16)


def on_device(
    tokens,
    captions,
    clip_groups,
    caption_groups,
    msg_weight,
    msg_gain,
    msg_in,
    msg_out,
    frame_gain,
    frame_in,
    frame_out,
    mlp_gain,
    up_weight,
    down_weight,
    proj_weight,
    out_cot,
):
    clips, frames, patches, width = tokens.shape
    seq = patches + 1
    cls_tokens = tokens[:, :, 0, :]
    message = jnp.einsum("cfd,de->cfe", cls_tokens, msg_weight, preferred_element_type=jnp.float32)
    msg_low, msg_hat, msg_rstd = norm_forward(message, msg_gain)
    msg_part, msg_kept = attn_forward(msg_low, msg_in, msg_out)
    message_next = message + lax.psum(msg_part, "mp")
    stream = jnp.concatenate([tokens.astype(jnp.float32), message_next[:, :, None, :]], axis=2)
    stream = stream.reshape(clips * frames, seq, width)
    frame_low, frame_hat, frame_rstd = norm_forward(stream, frame_gain)
    frame_part, frame_kept = attn_forward(frame_low, frame_in, frame_out)
    middle = stream + head_total(frame_part)
    mlp_low, mlp_hat, mlp_rstd = norm_forward(middle, mlp_gain)
    hidden = jnp.einsum("bsd,df->bsf", mlp_low, up_weight, preferred_element_type=jnp.float32)
    sigmo = jax.nn.sigmoid(1.702 * hidden)
    activ = (hidden * sigmo).astype(jnp.bfloat16)
    down_part = jnp.einsum("bsf,fd->bsd", activ, down_weight, preferred_element_type=jnp.float32)
    result = (middle + head_total(down_part)).reshape(clips, frames, seq, width)
    layer_out = result[:, :, :patches, :].astype(jnp.bfloat16)
    pooled_low = jnp.mean(result[:, :, 0, :], axis=1).astype(jnp.bfloat16)
    embed = jnp.dot(pooled_low, proj_weight, preferred_element_type=jnp.float32)
    embed_rinv = lax.rsqrt(jnp.sum(embed * embed, axis=-1, keepdims=True) + 1e-06)
    embed_low = (embed * embed_rinv).astype(jnp.bfloat16)
    caption_f = captions.astype(jnp.float32)
    caption_rinv = lax.rsqrt(jnp.sum(caption_f * caption_f, axis=-1, keepdims=True) + 1e-06)
    caption_low = (caption_f * caption_rinv).astype(jnp.bfloat16)
    normalized_text_vectors = caption_low.astype(jnp.float32)
    own_groups = caption_groups.astype(jnp.float32)
    clip_group_f = clip_groups.astype(jnp.float32)
    devices = lax.axis_size("dp")

    def block_scores(moving_caps):
        return softmax_sharpness_factor * jnp.dot(
            embed_low, moving_caps.astype(jnp.bfloat16).T, preferred_element_type=jnp.float32
        )

    def forward_step(step, state):
        row_stats, moving = state
        moving_caps, moving_groups = (moving[0], moving[1])
        scores = block_scores(moving_caps)
        positive = clip_group_f[:, None] == moving_groups[None, :]
        row_stats = combine(row_stats, block_stats(scores, positive, 1))
        column_stats = combine(moving[2:], block_stats(scores, positive, 0))
        moving = shifted(
            (
                moving_caps,
                moving_groups,
                column_stats[0],
                column_stats[1],
                column_stats[2],
                column_stats[3],
            ),
            "dp",
            1,
        )
        return (row_stats, moving)

    row_empty = jnp.full((clips,), lowest, jnp.float32)
    zero_rows = jnp.zeros((clips,), jnp.float32)
    start_rows = (row_empty, zero_rows, row_empty, zero_rows)
    start_moving = (normalized_text_vectors, own_groups, row_empty, zero_rows, row_empty, zero_rows)
    row_stats, home = lax.fori_loop(0, devices, forward_step, (start_rows, start_moving))
    row_lse = row_stats[0] + jnp.log(row_stats[1])
    row_plse = row_stats[2] + jnp.log(row_stats[3])
    column_lse = home[2] + jnp.log(home[3])
    column_plse = home[4] + jnp.log(home[5])
    local_loss = 0.5 * (jnp.sum(row_lse - row_plse) + jnp.sum(column_lse - column_plse))
    loss = lax.psum(local_loss, "dp")

    def backward_step(step, state):
        clip_vector_running_total, moving = state
        moving_caps, moving_groups, moving_lse, moving_plse, circulating_derivative = moving
        scores = block_scores(moving_caps)
        positive = clip_group_f[:, None] == moving_groups[None, :]
        dscore_low = score_grads(scores, positive, row_lse, row_plse, moving_lse, moving_plse)
        clip_vector_running_total = clip_vector_running_total + softmax_sharpness_factor * jnp.dot(
            dscore_low, moving_caps.astype(jnp.bfloat16), preferred_element_type=jnp.float32
        )
        circulating_derivative = circulating_derivative + softmax_sharpness_factor * jnp.dot(
            dscore_low.T, embed_low, preferred_element_type=jnp.float32
        )
        moving = shifted(
            (moving_caps, moving_groups, moving_lse, moving_plse, circulating_derivative), "dp", 1
        )
        return (clip_vector_running_total, moving)

    start_back = (
        normalized_text_vectors,
        own_groups,
        column_lse,
        column_plse,
        jnp.zeros_like(normalized_text_vectors),
    )
    embed_grad, back_home = lax.fori_loop(
        0, devices, backward_step, (jnp.zeros(embed.shape, jnp.float32), start_back)
    )
    caps_grad = back_home[4]
    caption_grad = caption_rinv * caps_grad - caption_f * caption_rinv**3 * jnp.sum(
        caption_f * caps_grad, axis=-1, keepdims=True
    )
    embed_diff = embed_rinv * embed_grad - embed * embed_rinv**3 * jnp.sum(
        embed * embed_grad, axis=-1, keepdims=True
    )
    embed_dlow = embed_diff.astype(jnp.bfloat16)
    proj_grad = jnp.dot(pooled_low.T, embed_dlow, preferred_element_type=jnp.float32)
    pooled_grad = jnp.dot(embed_dlow, proj_weight.T, preferred_element_type=jnp.float32)
    grad_stream = jnp.concatenate(
        [out_cot.astype(jnp.float32), jnp.zeros((clips, frames, 1, width), jnp.float32)], axis=2
    )
    grad_stream = grad_stream.at[:, :, 0, :].add(pooled_grad[:, None, :] / frames)
    grad_stream = grad_stream.reshape(clips * frames, seq, width)
    branch_low = grad_stream.astype(jnp.bfloat16)
    down_grad = jnp.einsum("bsf,bsd->fd", activ, branch_low, preferred_element_type=jnp.float32)
    activ_grad = jnp.einsum(
        "bsd,fd->bsf", branch_low, down_weight, preferred_element_type=jnp.float32
    )
    hidden_low = (activ_grad * (sigmo + 1.702 * hidden * sigmo * (1.0 - sigmo))).astype(
        jnp.bfloat16
    )
    up_grad = jnp.einsum("bsd,bsf->df", mlp_low, hidden_low, preferred_element_type=jnp.float32)
    mlp_normed_part = jnp.einsum(
        "bsf,df->bsd", hidden_low, up_weight, preferred_element_type=jnp.float32
    )
    mlp_normed_grad = head_total(mlp_normed_part)
    middle_part, mlp_gain_grad = norm_backward(mlp_normed_grad, mlp_gain, mlp_hat, mlp_rstd)
    middle_grad = grad_stream + middle_part
    frame_normed_part, frame_in_grad, frame_out_grad = attn_backward(
        frame_low, frame_in, frame_out, frame_kept, middle_grad.astype(jnp.bfloat16)
    )
    frame_normed_grad = head_total(frame_normed_part)
    stream_part, frame_gain_grad = norm_backward(
        frame_normed_grad, frame_gain, frame_hat, frame_rstd
    )
    stream_grad = (middle_grad + stream_part).reshape(clips, frames, seq, width)
    next_grad = stream_grad[:, :, patches, :]
    msg_normed_part, msg_in_grad, msg_out_grad = attn_backward(
        msg_low, msg_in, msg_out, msg_kept, next_grad.astype(jnp.bfloat16)
    )
    msg_normed_grad = lax.psum(msg_normed_part, "mp")
    message_part, msg_gain_grad = norm_backward(msg_normed_grad, msg_gain, msg_hat, msg_rstd)
    message_low = (next_grad + message_part).astype(jnp.bfloat16)
    msg_weight_grad = jnp.einsum(
        "cfd,cfe->de", cls_tokens, message_low, preferred_element_type=jnp.float32
    )
    cls_grad = jnp.einsum(
        "cfe,de->cfd", message_low, msg_weight, preferred_element_type=jnp.float32
    )
    token_grad = stream_grad[:, :, :patches, :].at[:, :, 0, :].add(cls_grad).astype(jnp.bfloat16)
    shares = (
        lax.psum_scatter(msg_weight_grad, "dp", scatter_dimension=0, tiled=True),
        lax.psum_scatter(msg_gain_grad, "dp", scatter_dimension=0, tiled=True),
        lax.psum_scatter(msg_in_grad, "dp", scatter_dimension=1, tiled=True),
        lax.psum_scatter(msg_out_grad, "dp", scatter_dimension=1, tiled=True),
        lax.psum_scatter(frame_gain_grad, "dp", scatter_dimension=0, tiled=True),
        lax.psum_scatter(frame_in_grad, "dp", scatter_dimension=1, tiled=True),
        lax.psum_scatter(frame_out_grad, "dp", scatter_dimension=1, tiled=True),
        lax.psum_scatter(mlp_gain_grad, "dp", scatter_dimension=0, tiled=True),
        lax.psum_scatter(up_grad, "dp", scatter_dimension=0, tiled=True),
        lax.psum_scatter(down_grad, "dp", scatter_dimension=1, tiled=True),
        lax.psum_scatter(proj_grad, "dp", scatter_dimension=0, tiled=True),
    )
    msg_weight_share, msg_gain_share, msg_in_share, msg_out_share = (
        shares[0],
        shares[1],
        shares[2],
        shares[3],
    )
    frame_gain_share, frame_in_share, frame_out_share = (shares[4], shares[5], shares[6])
    mlp_gain_share, up_share, down_share, proj_share = (shares[7], shares[8], shares[9], shares[10])
    return (
        layer_out,
        loss,
        token_grad,
        caption_grad,
        msg_weight_share,
        msg_gain_share,
        msg_in_share,
        msg_out_share,
        frame_gain_share,
        frame_in_share,
        frame_out_share,
        mlp_gain_share,
        up_share,
        down_share,
        proj_share,
    )


def solution(mesh):
    in_specs = (
        P("dp", None, None, None),
        P("dp", None),
        P("dp"),
        P("dp"),
        P(),
        P(),
        P(None, None, "mp"),
        P("mp", None),
        P(),
        P(None, None, "mp"),
        P("mp", None),
        P(),
        P(None, "mp"),
        P("mp", None),
        P(),
        P("dp", None, None, None),
    )
    out_specs = (
        P("dp", None, None, None),
        P(),
        P("dp", None, None, None),
        P("dp", None),
        P("dp", None),
        P("dp"),
        P(None, "dp", "mp"),
        P("mp", "dp"),
        P("dp"),
        P(None, "dp", "mp"),
        P("mp", "dp"),
        P("dp"),
        P("dp", "mp"),
        P("mp", "dp"),
        P("dp", None),
    )
    return jax.shard_map(
        on_device, mesh=mesh, in_specs=in_specs, out_specs=out_specs, check_vma=False
    )
```

profile of v0, /device:TPU:0, one launch (start us, length us, event | category | flops | bytes accessed | tf_op | source)
XLA Modules:
  0.0 2061.5 jit_solution(13158390950665891793)
XLA Ops:
  7.3 4.4 convert_element_type.167
  15.5 9.9 psum.21
  32.1 3.9 convert_bitcast_fusion
  58.8 5.0 fusion.63
  65.3 121.2 %all-reduce.18.cloned.1.call-done = f32[8,198,768]{2,0,1:T(8,128)} async-done(((f32[8,198,768]{2,0,1:T(8,128)}), f32[8,198,768]{2,0,1:T(8,128)}) %all-reduce.18.cloned.1.call-update) | async-done | bytes 4866064
  191.3 65.3 %all-gather.5.cloned.1.call-done = f32[8,198,768]{2,1,0:T(8,128)} async-done(((f32[4,198,768]{2,1,0:T(8,128)}), f32[8,198,768]{2,1,0:T(8,128)}) %all-gather.5.cloned.1.call-update) | async-done | bytes 4866064 | tf_op jit(solution)/shard_map/all_gather | solution.py:20
  256.6 5.5 fusion.106
  264.3 7.2 multiply_convert_fusion.2
  273.7 7.6 fusion.6
  281.4 122.5 %all-reduce.20.cloned.1.call-done = f32[8,198,768]{2,0,1:T(8,128)} async-done(((f32[8,198,768]{2,0,1:T(8,128)}), f32[8,198,768]{2,0,1:T(8,128)}) %all-reduce.20.cloned.1.call-update) | async-done | bytes 4866064
  418.7 55.2 %all-gather.7.cloned.1.call-done = f32[8,198,768]{2,1,0:T(8,128)} async-done(((f32[4,198,768]{2,1,0:T(8,128)}), f32[8,198,768]{2,1,0:T(8,128)}) %all-gather.7.cloned.1.call-update) | async-done | bytes 4866064 | tf_op jit(solution)/shard_map/all_gather | solution.py:20
  474.0 5.6 fusion.8
  483.5 253.0 %while.51 = (s32[]{:T(128)}, f32[1]{0:T(128)}, f32[1]{0:T(128)}, f32[1]{0:T(128)}, f32[1]{0:T(128)}, /*index=5*/bf16[1,512]{1,0:T(2,128)(2,1)S(1)}, f32[1]{0:T(1...) while((s32[]{:T(128)}, f32[1]{0:T(128)}, f32[1]{0:T(128)}, ...), condition=%wide.region_17.18_spmd, body=%wide.region_16.17_spmd.sunk | while | flops 2079 | bytes 13258 | solution.py:211
  550.3 3.7 collective-permute-start.3
  613.5 3.7 collective-permute-start.3
  736.7 212.8 %while.52 = (s32[]{:T(128)}, f32[1,512]{1,0:T(1,128)S(1)}, bf16[1,512]{1,0:T(2,128)(2,1)S(1)}, f32[1]{0:T(128)}, f32[1]{0:T(128)}, /*index=5*/f32[1]{0:T(128)}, ...) while((s32[]{:T(128)}, f32[1,512]{1,0:T(1,128)S(1)}, ...), condition=%wide.region_20.0_spmd.clone, body=%wide.region_19.0_spmd.clone.sunk | while | flops 6671 | bytes 39544 | solution.py:243
  738.5 3.9 collective-permute-start.9
  744.3 5.4 collective-permute-done.10
  759.1 3.7 collective-permute-done.10
  772.2 3.7 collective-permute-done.10
  791.7 3.9 collective-permute-start.9
  797.4 5.4 collective-permute-done.10
  812.3 3.7 collective-permute-done.10
  825.3 3.7 collective-permute-done.10
  844.9 3.9 collective-permute-start.9
  850.6 5.4 collective-permute-done.10
  865.4 3.7 collective-permute-done.10
  878.5 3.7 collective-permute-done.10
  898.0 3.9 collective-permute-start.9
  903.8 5.4 collective-permute-done.10
  918.6 3.7 collective-permute-done.10
  931.7 3.7 collective-permute-done.10
  955.1 9.4 multiply_convert_fusion.1
  966.8 7.7 fusion.10
  974.5 121.5 %all-reduce.22.cloned.1.call-done = f32[8,198,768]{2,0,1:T(8,128)} async-done(((f32[8,198,768]{2,0,1:T(8,128)}), f32[8,198,768]{2,0,1:T(8,128)}) %all-reduce.22.cloned.1.call-update) | async-done | bytes 4866064
  1101.0 65.1 %all-gather.9.cloned.1.call-done = f32[8,198,768]{2,1,0:T(8,128)} async-done(((f32[4,198,768]{2,1,0:T(8,128)}), f32[8,198,768]{2,1,0:T(8,128)}) %all-gather.9.cloned.1.call-update) | async-done | bytes 4866064 | tf_op jit(solution)/shard_map/all_gather | solution.py:20
  1166.1 9.8 multiply_reduce_fusion.2
  1176.0 6.6 fusion.105
  1187.2 7.5 convolution_convert_fusion
  1194.7 7.7 multiply_reduce_fusion
  1202.4 11.4 multiply_convert_fusion
  1213.9 5.8 multiply_convert_fusion.5
  1231.2 5.5 fusion.28
  1236.8 122.5 %all-reduce.24.cloned.1.call-done = f32[8,198,768]{2,0,1:T(8,128)} async-done(((f32[8,198,768]{2,0,1:T(8,128)}), f32[8,198,768]{2,0,1:T(8,128)}) %all-reduce.24.cloned.1.call-update) | async-done | bytes 4866064
  1364.5 8.1 fusion.40
  1372.6 6.6 copy.162
  1379.2 50.2 %all-gather.11.cloned.1.call-done = f32[8,198,768]{2,1,0:T(8,128)} async-done(((f32[4,198,768]{2,1,0:T(8,128)}), f32[8,198,768]{2,1,0:T(8,128)}) %all-gather.11.cloned.1.call-update) | async-done | bytes 4866064 | tf_op jit(solution)/shard_map/all_gather | solution.py:20
  1429.4 10.0 multiply_reduce_fusion.3
  1439.5 6.0 add_bitcast_fusion
  1451.6 6.2 copy.159
  1459.5 9.8 fusion.14
  1469.4 10.1 convolution_bitcast_fusion
  1479.5 5.3 fusion.48
  1487.7 7.3 psum.23
  1499.9 4.2 slice.137
  1506.0 62.4 %all-reduce.10 = (f32[]{:T(128)}, f32[768]{0:T(1024)S(1)}, f32[768]{0:T(1024)S(1)}, f32[768]{0:T(1024)S(1)}) all-reduce(f32[]{:T(128)} %bitcast.32, f32[768]{0:T(1024)S(1)} %get-tuple-element.268, f32[768]{0:T(1024)S(1)} %copy-done.62, f32[768]{0:T(1024)S(1)} %copy-done.61), channel_id=1, replica_groups=mesh['dp'=16,'mp'=2] {'dp'}, use_global_device_ids=true, to_apply=%region_18.19 | all-reduce | flops 2305 | bytes 18440 | tf_op jit(solution)/shard_map/psum | solution.py:217
  1568.4 4.1 slice.112
  1576.5 67.1 %all-reduce.26.cloned.1.call-done = (f32[3,768,384]{2,0,1:T(4,128)}, f32[3,768,384]{2,0,1:T(4,128)}) async-done(((f32[3,768,384]{2,0,1:T(4,128)}, f32[3,768,384]{2,0,1:T(4,128)}), (f32[3,768,384]{2,0,1:T(4,128)}, f32[3,768,384]{2,0,1:T(4,128)})) %all-reduce.26.cloned.1.call-update) | async-done | bytes 7077904
  1647.0 60.7 %reduce-scatter.21.cloned.1.call-done = f32[48,512]{1,0:T(8,128)} async-done(((f32[768,512]{1,0:T(8,128)}), f32[48,512]{1,0:T(8,128)}) %reduce-scatter.21.cloned.1.call-update) | async-done | bytes 98320 | tf_op jit(solution)/shard_map/reduce_scatter | solution.py:309
  1707.7 79.1 %reduce-scatter.17.cloned.1.call-done = f32[48,1536]{1,0:T(8,128)} async-done(((f32[768,1536]{1,0:T(8,128)}), f32[48,1536]{1,0:T(8,128)}) %reduce-scatter.17.cloned.1.call-update) | async-done | bytes 294928 | tf_op jit(solution)/shard_map/reduce_scatter | solution.py:307
  1786.8 79.4 %reduce-scatter.19.cloned.1.call-done = f32[1536,48]{0,1:T(8,128)} async-done(((f32[1536,768]{0,1:T(8,128)}), f32[1536,48]{0,1:T(8,128)}) %reduce-scatter.19.cloned.1.call-update) | async-done | bytes 294928 | tf_op jit(solution)/shard_map/reduce_scatter | solution.py:308
  1866.2 61.3 %reduce-scatter.15.cloned.1.call-done = f32[384,48]{0,1:T(8,128)} async-done(((f32[384,768]{0,1:T(8,128)}), f32[384,48]{0,1:T(8,128)}) %reduce-scatter.15.cloned.1.call-update) | async-done | bytes 73744 | tf_op jit(solution)/shard_map/reduce_scatter | solution.py:305
  1927.4 61.1 %reduce-scatter.13.cloned.1.call-done = f32[384,48]{0,1:T(8,128)} async-done(((f32[384,768]{0,1:T(8,128)}), f32[384,48]{0,1:T(8,128)}) %reduce-scatter.13.cloned.1.call-update) | async-done | bytes 73744 | tf_op jit(solution)/shard_map/reduce_scatter | solution.py:302
  1988.6 66.2 %reduce-scatter.23.cloned.1.call-done = f32[48,768]{1,0:T(8,128)} async-done(((f32[768,768]{1,0:T(8,128)}), f32[48,768]{1,0:T(8,128)}) %reduce-scatter.23.cloned.1.call-update) | async-done | bytes 147472
  (817 shorter events, 394.9 us)
Async XLA Ops:
  7.2 179.4 %all-reduce.18.cloned.1.call-start = ((), (), s32[]{:S(2)}) async-start(), calls=%async_computation.16 | async-start | bytes 9732096
  63.8 192.8 %all-gather.5.cloned.1.call-start = ((), (), s32[]{:S(2)}) async-start(), calls=%async_computation.6 | async-start | bytes 7372800 | tf_op jit(solution)/shard_map/all_gather | solution.py:20
  191.3 212.6 %all-reduce.20.cloned.1.call-start = ((), (), s32[]{:S(2)}) async-start(), calls=%async_computation.17 | async-start | bytes 9732096
  281.3 192.6 %all-gather.7.cloned.1.call-start = ((), (), s32[]{:S(2)}) async-start(), calls=%async_computation.7 | async-start | bytes 7372800 | tf_op jit(solution)/shard_map/all_gather | solution.py:20
  408.6 687.4 %all-reduce.22.cloned.1.call-start = ((), (), s32[]{:S(2)}) async-start(), calls=%async_computation.18 | async-start | bytes 9732096
  483.5 14.1 collective-permute-start
  483.6 8.4 collective-permute-start.1
  487.3 6.9 collective-permute-start.2
  500.9 12.3 collective-permute-start
  501.0 6.6 collective-permute-start.1
  516.5 12.3 collective-permute-start
  516.6 6.6 collective-permute-start.1
  532.1 11.4 collective-permute-start
  546.8 14.0 collective-permute-start
  546.9 8.3 collective-permute-start.1
  549.1 7.0 collective-permute-start.2
  564.1 12.3 collective-permute-start
  579.7 12.3 collective-permute-start
  579.8 6.6 collective-permute-start.1
  595.3 11.4 collective-permute-start
  610.0 14.0 collective-permute-start
  610.1 8.3 collective-permute-start.1
  612.3 7.0 collective-permute-start.2
  627.4 12.3 collective-permute-start
  643.0 12.3 collective-permute-start
  643.0 6.6 collective-permute-start.1
  658.6 11.4 collective-permute-start
  673.3 14.0 collective-permute-start
  673.4 8.3 collective-permute-start.1
  675.6 7.0 collective-permute-start.2
  690.6 12.3 collective-permute-start
  706.2 12.3 collective-permute-start
  706.3 6.6 collective-permute-start.1
  721.8 11.4 collective-permute-start
  736.7 7.5 collective-permute-start.6
  736.8 7.2 collective-permute-start.7
  751.5 7.5 collective-permute-start.6
  764.6 7.5 collective-permute-start.6
  777.7 7.5 collective-permute-start.6
  789.9 7.5 collective-permute-start.6
  790.0 7.2 collective-permute-start.7
  804.7 7.5 collective-permute-start.6
  817.8 7.5 collective-permute-start.6
  830.9 7.5 collective-permute-start.6
  843.1 7.5 collective-permute-start.6
  843.2 7.2 collective-permute-start.7
  857.9 7.5 collective-permute-start.6
  871.0 7.5 collective-permute-start.6
  884.1 7.5 collective-permute-start.6
  896.3 7.5 collective-permute-start.6
  896.3 7.2 collective-permute-start.7
  911.1 7.5 collective-permute-start.6
  924.2 7.5 collective-permute-start.6
  937.3 7.5 collective-permute-start.6
  974.5 191.6 %all-gather.9.cloned.1.call-start = ((), (), s32[]{:S(2)}) async-start(), calls=%async_computation.8 | async-start | bytes 7372800 | tf_op jit(solution)/shard_map/all_gather | solution.py:20
  1100.7 258.5 %all-reduce.24.cloned.1.call-start = ((), (), s32[]{:S(2)}) async-start(), calls=%async_computation.19 | async-start | bytes 9732096
  1236.7 192.7 %all-gather.11.cloned.1.call-start = ((), (), s32[]{:S(2)}) async-start(), calls=%async_computation.9 | async-start | bytes 7372800 | tf_op jit(solution)/shard_map/all_gather | solution.py:20
  1364.0 279.6 %all-reduce.26.cloned.1.call-start = ((), (), s32[]{:S(2)}) async-start(), calls=%async_computation.20 | async-start | bytes 18874368
  1457.8 249.9 %reduce-scatter.21.cloned.1.call-start = ((), (), s32[]{:S(2)}) async-start(), calls=%async_computation.14 | async-start | bytes 1671168 | tf_op jit(solution)/shard_map/reduce_scatter | solution.py:309
  1459.3 327.5 %reduce-scatter.17.cloned.1.call-start = ((), (), s32[]{:S(2)}) async-start(), calls=%async_computation.12 | async-start | bytes 5013504 | tf_op jit(solution)/shard_map/reduce_scatter | solution.py:307
  1469.3 396.8 %reduce-scatter.19.cloned.1.call-start = ((), (), s32[]{:S(2)}) async-start(), calls=%async_computation.13 | async-start | bytes 5013504 | tf_op jit(solution)/shard_map/reduce_scatter | solution.py:308
  1479.5 448.0 %reduce-scatter.15.cloned.1.call-start = ((), (), s32[]{:S(2)}) async-start(), calls=%async_computation.11 | async-start | bytes 1253376 | tf_op jit(solution)/shard_map/reduce_scatter | solution.py:305
  1484.9 503.7 %reduce-scatter.13.cloned.1.call-start = ((), (), s32[]{:S(2)}) async-start(), calls=%async_computation.10 | async-start | bytes 1253376 | tf_op jit(solution)/shard_map/reduce_scatter | solution.py:302
  1487.1 567.7 %reduce-scatter.23.cloned.1.call-start = ((), (), s32[]{:S(2)}) async-start(), calls=%async_computation.15 | async-start | bytes 2506752
  (202 other events, 2718.7 us)
Sparse Core Ops, SparseCore 0:
  64.0 122.5 all-reduce.17
  191.4 65.2 all-gather.4
  281.5 122.3 all-reduce.19
  408.7 65.2 all-gather.6
  974.6 121.3 all-reduce.21
  1100.9 65.2 all-gather.8
  1236.8 122.3 all-reduce.23
  1364.1 65.2 all-gather.10
  1458.0 185.6 all-reduce.25
  1648.1 59.5 reduce-scatter.20
  1712.2 74.5 reduce-scatter.16
  1791.6 74.5 reduce-scatter.18
  1870.3 57.0 reduce-scatter.14
  1931.5 57.0 reduce-scatter.12
  1992.8 61.9 reduce-scatter.22
where the time goes:
time: 2070 us; the launch traced here: 2060 us
  waiting for transfers between devices  1360 us (66%)
  starting transfers between devices  171 us (8%)
  matrix products  123 us (6%)
  loops' own time  114 us (6%)
  other arithmetic  104 us (5%)
  local copies, waits for them, and re-layouts  91.2 us (4%)
  blocking collectives  79.6 us (4%)
    unnamed x21, waiting for transfers between devices  621 us
    all_gather x4, waiting for transfers between devices, head_total(): return lax.all_gather(share, 'mp', axis=0, tiled=True)  236 us
    ppermute x176, starting transfers between devices, shifted(): lax.ppermute(value, axis, [(i, (i + by) % size) for i in range(size)])  169 us
    ppermute x176, waiting for transfers between devices, shifted(): lax.ppermute(value, axis, [(i, (i + by) % size) for i in range(size)])  160 us
    reduce_scatter x1, waiting for transfers between devices, on_device(): lax.psum_scatter(down_grad, 'dp', scatter_dimension=1, tiled=True)  79.4 us
    reduce_scatter x1, waiting for transfers between devices, on_device(): lax.psum_scatter(up_grad, 'dp', scatter_dimension=0, tiled=True)  79.1 us
    another operation x1, loops' own time, on_device(): lax.fori_loop(0, devices, forward_step, (start_rows, start_moving))  69.9 us
    psum x1, blocking collectives, on_device(): loss = lax.psum(local_loss, 'dp')  62.4 us
  transfers between devices with their start and end apart: 191, of which 131 were waited for; matrix products, arithmetic and copies ran while one was open for 5% of the time, Pallas kernels for 0%

commit v1 on v0

v1 whole, which is shorter than its diff:
```python
import jax
import jax.numpy as jnp
from jax import lax
from jax.sharding import PartitionSpec as P

HEADS = 12
SHARPNESS = 50.0
LOWEST = -1e30
BF = jnp.bfloat16
F32 = jnp.float32


def swap(value):
    return lax.ppermute(value, "mp", [(0, 1), (1, 0)])


def flip(value, bit):
    size = lax.axis_size("dp")
    return lax.ppermute(value, "dp", [(i, i ^ bit) for i in range(size)])


def bits_of(size):
    bits = []
    bit = 1
    while bit < size:
        bits.append(bit)
        bit *= 2
    return bits


def row_order(size):
    bits = bits_of(size)
    order = []
    for p in range(size):
        mask = 0
        for k, bit in enumerate(bits):
            if (p >> (len(bits) - 1 - k)) & 1:
                mask |= bit
        order.append(mask)
    return order


def own_first(rows_first):
    size = lax.axis_size("dp")
    me = lax.axis_index("dp")
    blocks = rows_first.reshape((size, rows_first.shape[0] // size) + rows_first.shape[1:])
    order = jnp.bitwise_xor(jnp.asarray(row_order(size), jnp.int32), me)
    return jnp.take(blocks, order, axis=0).reshape(rows_first.shape)


def halve(value, bit, dtype=BF):
    rows = value.shape[-2] // 2
    keep, send = value[..., :rows, :], value[..., rows:, :]
    got = flip(send, bit)
    return (keep.astype(F32) + got.astype(F32)).astype(dtype)


def reduce_rows(value):
    bits = bits_of(lax.axis_size("dp"))
    value = halve(value, bits[0])
    value = (value[0].astype(F32) + swap(value[1]).astype(F32)).astype(BF)
    for bit in bits[1:-1]:
        value = halve(value, bit)
    return halve(value, bits[-1], F32)


def norm_forward(value, gain):
    centered = value - jnp.mean(value, axis=-1, keepdims=True)
    rstd = lax.rsqrt(jnp.mean(centered * centered, axis=-1, keepdims=True) + 1e-05)
    normal = centered * rstd
    return ((normal * gain).astype(BF), normal, rstd)


def norm_backward(grad, gain, normal, rstd):
    scaled = grad * gain
    inner = (
        scaled
        - jnp.mean(scaled, axis=-1, keepdims=True)
        - normal * jnp.mean(scaled * normal, axis=-1, keepdims=True)
    )
    gain_grad = jnp.sum((grad * normal).reshape(-1, grad.shape[-1]), axis=0)
    return (rstd * inner, gain_grad)


def dot(a, b):
    return jnp.dot(a, b, preferred_element_type=F32)


def attn_forward(normed, w_in, w_out, valid):
    batch, length, width = normed.shape
    head_size = width // HEADS
    local = w_in.shape[2]
    packed = jnp.einsum("bsd,kde->kbse", normed, w_in, preferred_element_type=F32).astype(BF)
    shape = (batch, length, local // head_size, head_size)
    query, keys, values = (packed[k].reshape(shape) for k in range(3))
    scores = jnp.einsum("bqhe,bkhe->bhqk", query, keys, preferred_element_type=F32) * head_size ** (-0.5)
    if valid < length:
        scores = jnp.where(jnp.arange(length) < valid, scores, LOWEST)
    top = jnp.max(scores, axis=-1, keepdims=True)
    logsum = top + jnp.log(jnp.sum(jnp.exp(scores - top), axis=-1, keepdims=True))
    weights = jnp.exp(scores - logsum).astype(BF)
    context = jnp.einsum("bhqk,bkhe->bqhe", weights, values, preferred_element_type=F32)
    context = context.reshape(batch, length, local).astype(BF)
    branch = jnp.einsum("bse,ed->bsd", context, w_out, preferred_element_type=F32)
    return (branch, (query, keys, values, logsum, context))


def attn_backward(w_in, w_out, kept, grad_low, valid):
    query, keys, values, logsum, context = kept
    batch, length, heads, head_size = query.shape
    scale = head_size ** (-0.5)
    context_grad = jnp.einsum("bsd,ed->bse", grad_low, w_out, preferred_element_type=F32)
    context_grad = context_grad.astype(BF).reshape(batch, length, heads, head_size)
    scores = jnp.einsum("bqhe,bkhe->bhqk", query, keys, preferred_element_type=F32) * scale
    if valid < length:
        scores = jnp.where(jnp.arange(length) < valid, scores, LOWEST)
    weights = jnp.exp(scores - logsum)
    weight_grad = jnp.einsum("bqhe,bkhe->bhqk", context_grad, values, preferred_element_type=F32)
    value_grad = jnp.einsum("bhqk,bqhe->bkhe", weights.astype(BF), context_grad, preferred_element_type=F32)
    score_grad = (weights * (weight_grad - jnp.sum(weights * weight_grad, axis=-1, keepdims=True))).astype(BF)
    query_grad = jnp.einsum("bhqk,bkhe->bqhe", score_grad, keys, preferred_element_type=F32) * scale
    key_grad = jnp.einsum("bhqk,bqhe->bkhe", score_grad, query, preferred_element_type=F32) * scale
    stacked = (
        jnp.stack([query_grad, key_grad, value_grad]).reshape(3, batch, length, heads * head_size).astype(BF)
    )
    normed_grad = jnp.einsum("kbse,kde->bsd", stacked, w_in, preferred_element_type=F32)
    return (normed_grad, stacked)


def contrast(pooled_all, captions_all, clip_groups, caption_groups, proj_weight):
    embed = dot(pooled_all, proj_weight)
    embed_rinv = lax.rsqrt(jnp.sum(embed * embed, axis=-1, keepdims=True) + 1e-06)
    embed_low = (embed * embed_rinv).astype(BF)
    caption_f = captions_all.astype(F32)
    caption_rinv = lax.rsqrt(jnp.sum(caption_f * caption_f, axis=-1, keepdims=True) + 1e-06)
    caption_low = (caption_f * caption_rinv).astype(BF)
    scores = SHARPNESS * dot(embed_low, caption_low.T)
    positive = clip_groups[:, None] == caption_groups[None, :]
    masked = jnp.where(positive, scores, LOWEST)

    def side(axis):
        top = jnp.max(scores, axis=axis, keepdims=True)
        each = jnp.exp(scores - top)
        total = jnp.sum(each, axis=axis, keepdims=True)
        pos_top = jnp.max(masked, axis=axis, keepdims=True)
        pos_each = jnp.where(positive, jnp.exp(masked - pos_top), 0.0)
        pos_total = jnp.sum(pos_each, axis=axis, keepdims=True)
        part = jnp.sum(top + jnp.log(total) - pos_top - jnp.log(pos_total))
        return (part, each / total - pos_each / pos_total)

    row_loss, row_grad = side(1)
    column_loss, column_grad = side(0)
    loss = 0.5 * (row_loss + column_loss)
    dscore = (0.5 * (row_grad + column_grad)).astype(BF)
    embed_grad = SHARPNESS * dot(dscore, caption_low)
    caps_grad = SHARPNESS * dot(dscore.T, embed_low)
    caption_grad = caption_rinv * caps_grad - caption_f * caption_rinv**3 * jnp.sum(
        caption_f * caps_grad, axis=-1, keepdims=True
    )
    embed_diff = embed_rinv * embed_grad - embed * embed_rinv**3 * jnp.sum(
        embed * embed_grad, axis=-1, keepdims=True
    )
    return (loss, caption_grad, embed_diff.astype(BF))


def on_device(
    tokens,
    captions,
    clip_groups,
    caption_groups,
    msg_weight,
    msg_gain,
    msg_in,
    msg_out,
    frame_gain,
    frame_in,
    frame_out,
    mlp_gain,
    up_weight,
    down_weight,
    proj_weight,
    out_cot,
):
    clips, frames, patches, width = tokens.shape
    valid = patches + 1
    seq = -(-valid // 16) * 16
    half = frames // lax.axis_size("mp")
    me_dp, me_mp = (lax.axis_index("dp"), lax.axis_index("mp"))
    share = width // lax.axis_size("dp")

    def gather(value):
        return lax.all_gather(value, "dp", axis=0, tiled=True)

    def mine(value, axis=1):
        return lax.dynamic_slice_in_dim(value, me_dp * share, share, axis)

    def own(value):
        return lax.dynamic_slice_in_dim(value, me_mp * half, half, 1)

    def both(value):
        other = swap(value)
        first = jnp.where(me_mp == 0, value, other)
        second = jnp.where(me_mp == 0, other, value)
        return jnp.concatenate([first, second], axis=1)

    w_in = jnp.concatenate([frame_in, swap(frame_in)], axis=2)
    w_out = jnp.concatenate([frame_out, swap(frame_out)], axis=0)
    w_up = jnp.concatenate([up_weight, swap(up_weight)], axis=1)
    w_down = jnp.concatenate([down_weight, swap(down_weight)], axis=0)

    cls_tokens = tokens[:, :, 0, :]
    message = jnp.einsum("cfd,de->cfe", cls_tokens, msg_weight, preferred_element_type=F32)
    msg_low, msg_hat, msg_rstd = norm_forward(message, msg_gain)
    msg_part, msg_kept = attn_forward(msg_low, msg_in, msg_out, frames)
    message_next = message + (msg_part + swap(msg_part))

    pad = jnp.zeros((clips, half, seq - valid, width), F32)
    stream = jnp.concatenate([own(tokens).astype(F32), own(message_next)[:, :, None, :], pad], axis=2)
    stream = stream.reshape(clips * half, seq, width)
    frame_low, frame_hat, frame_rstd = norm_forward(stream, frame_gain)
    branch, frame_kept = attn_forward(frame_low, w_in, w_out, valid)
    middle = stream + branch
    mlp_low, mlp_hat, mlp_rstd = norm_forward(middle, mlp_gain)
    rows = clips * half * seq
    mlp_low = mlp_low.reshape(rows, width)
    hidden = dot(mlp_low, w_up)
    sigmo = jax.nn.sigmoid(1.702 * hidden)
    activ = (hidden * sigmo).astype(BF)
    slope = sigmo + 1.702 * hidden * sigmo * (1.0 - sigmo)
    result = (middle + dot(activ, w_down).reshape(middle.shape)).reshape(clips, half, seq, width)
    layer_out = both(result[:, :, :patches, :].astype(BF))

    pooled = jnp.sum(result[:, :, 0, :], axis=1)
    pooled_low = ((pooled + swap(pooled)) / frames).astype(BF)
    pooled_all = gather(pooled_low)
    ids = jnp.stack([clip_groups, caption_groups], axis=1)
    ids_all = gather(ids)
    loss, caption_grad_all, embed_dlow = contrast(
        pooled_all, gather(captions), ids_all[:, 0], ids_all[:, 1], proj_weight
    )
    caption_grad = lax.dynamic_slice_in_dim(caption_grad_all, me_dp * clips, clips, 0)
    proj_share = dot(mine(pooled_all).T, embed_dlow)
    embed_own = lax.dynamic_slice_in_dim(embed_dlow, me_dp * clips, clips, 0)
    pooled_grad = dot(embed_own, proj_weight.T)

    grad_stream = jnp.concatenate(
        [own(out_cot).astype(F32), jnp.zeros((clips, half, seq - patches, width), F32)], axis=2
    )
    grad_stream = grad_stream.at[:, :, 0, :].add(pooled_grad[:, None, :] / frames)
    grad_low = grad_stream.astype(BF).reshape(rows, width)
    grad_stream = grad_stream.reshape(clips * half, seq, width)
    f_half = w_up.shape[1] // 2

    def columns(value):
        return jnp.stack([value[:, : value.shape[1] // 2], value[:, value.shape[1] // 2 :]])

    down_t = jnp.einsum("dr,mrf->mdf", own_first(grad_low.T), columns(activ), preferred_element_type=F32)
    down_share = reduce_rows(down_t.astype(BF)).T
    hidden_low = (dot(grad_low, w_down.T) * slope).astype(BF)
    up_grad = jnp.einsum("dr,mrf->mdf", own_first(mlp_low.T), columns(hidden_low), preferred_element_type=F32)
    up_share = reduce_rows(up_grad.astype(BF))
    mlp_normed_grad = dot(hidden_low, w_up.T).reshape(middle.shape)
    middle_part, mlp_gain_grad = norm_backward(mlp_normed_grad, mlp_gain, mlp_hat, mlp_rstd)
    middle_grad = grad_stream + middle_part
    middle_low = middle_grad.astype(BF)
    frame_normed_grad, stacked = attn_backward(w_in, w_out, frame_kept, middle_low, valid)
    stream_part, frame_gain_grad = norm_backward(frame_normed_grad, frame_gain, frame_hat, frame_rstd)
    stream_grad = (middle_grad + stream_part).reshape(clips, half, seq, width)
    h_half = w_in.shape[2] // 2
    stacked = stacked.reshape(3, rows, 2, h_half).transpose(2, 1, 0, 3).reshape(2, rows, 3 * h_half)
    in_grad = jnp.einsum(
        "dr,mrf->mdf", own_first(frame_low.reshape(rows, width).T), stacked, preferred_element_type=F32
    )
    in_share = reduce_rows(in_grad.astype(BF)).reshape(share, 3, h_half).transpose(1, 0, 2)
    out_t = jnp.einsum(
        "dr,mrf->mdf",
        own_first(middle_low.reshape(rows, width).T),
        columns(frame_kept[4].reshape(rows, width)),
        preferred_element_type=F32,
    )
    out_share = reduce_rows(out_t.astype(BF)).T

    next_grad = both(stream_grad[:, :, patches, :])
    next_low = next_grad.astype(BF)
    msg_normed_part, msg_stacked = attn_backward(msg_in, msg_out, msg_kept, next_low, frames)
    msg_normed_grad = msg_normed_part + swap(msg_normed_part)
    message_part, msg_gain_grad = norm_backward(msg_normed_grad, msg_gain, msg_hat, msg_rstd)
    message_low = (next_grad + message_part).astype(BF)
    cls_grad = jnp.einsum("cfe,de->cfd", message_low, msg_weight, preferred_element_type=F32)
    token_own = stream_grad[:, :, :patches, :].at[:, :, 0, :].add(own(cls_grad)).astype(BF)
    token_grad = both(token_own)

    def flat(value):
        return value.reshape(clips * frames, value.shape[-1])

    factors = jnp.concatenate(
        [
            flat(cls_tokens),
            flat(message_low),
            flat(msg_low),
            flat(msg_stacked.transpose(1, 2, 0, 3).reshape(clips, frames, -1)),
            flat(msg_kept[4]),
            flat(next_low),
        ],
        axis=1,
    )
    factors = gather(factors)
    at = 0
    parts = []
    for wide in (width, width, width, 3 * h_half, h_half, width):
        parts.append(factors[:, at : at + wide])
        at += wide
    msg_weight_share = dot(mine(parts[0]).T, parts[1])
    msg_in_share = dot(mine(parts[2]).T, parts[3]).reshape(share, 3, h_half).transpose(1, 0, 2)
    msg_out_share = dot(parts[4].T, mine(parts[5]))
    gains = jnp.stack([mlp_gain_grad, frame_gain_grad])
    gains = gains + swap(gains)
    gains = jnp.concatenate([gains, msg_gain_grad[None]], axis=0)
    gains = jnp.sum(gather(gains[None]), axis=0)
    gains = mine(gains)
    return (
        layer_out,
        loss,
        token_grad,
        caption_grad,
        msg_weight_share,
        gains[2],
        msg_in_share,
        msg_out_share,
        gains[1],
        in_share,
        out_share,
        gains[0],
        up_share,
        down_share,
        proj_share,
    )


def solution(mesh):
    in_specs = (
        P("dp", None, None, None),
        P("dp", None),
        P("dp"),
        P("dp"),
        P(),
        P(),
        P(None, None, "mp"),
        P("mp", None),
        P(),
        P(None, None, "mp"),
        P("mp", None),
        P(),
        P(None, "mp"),
        P("mp", None),
        P(),
        P("dp", None, None, None),
    )
    out_specs = (
        P("dp", None, None, None),
        P(),
        P("dp", None, None, None),
        P("dp", None),
        P("dp", None),
        P("dp"),
        P(None, "dp", "mp"),
        P("mp", "dp"),
        P("dp"),
        P(None, "dp", "mp"),
        P("mp", "dp"),
        P("dp"),
        P("dp", "mp"),
        P("mp", "dp"),
        P("dp", None),
    )
    return jax.shard_map(
        on_device, mesh=mesh, in_specs=in_specs, out_specs=out_specs, check_vma=False
    )
```

time: 2070 us -> 586 us (0.28)
  waiting for transfers between devices: 1360 us -> 122 us
  starting transfers between devices: 171 us -> 20.5 us
  loops' own time: 114 us -> 0 us
  local copies, waits for them, and re-layouts: 91.2 us -> 139 us
    unnamed x21 -> x1, waiting for transfers between devices: 621 us -> 0.02 us
    reduce_scatter x5 -> x0, waiting for transfers between devices: 342 us -> none  [the longest x1 79.4 us: on_device(): lax.psum_scatter(down_grad, 'dp', scatter_dimension=1, tiled=True)]
    all_gather x4 -> x1, waiting for transfers between devices: 236 us -> 0.01 us  [gather(): return lax.all_gather(value, 'dp', axis=0, tiled=True)]
    ppermute x176 -> x31, starting transfers between devices: 169 us -> 20.5 us  [the longest x15 18.5 us: swap(): return lax.ppermute(value, 'mp', [(0, 1), (1, 0)])]
    another operation x2 -> x0, loops' own time: 114 us -> none  [the longest x1 69.9 us: on_device(): lax.fori_loop(0, devices, forward_step, (start_rows, start_moving))]
    psum x3 -> x0, blocking collectives: 79.6 us -> none  [the longest x1 62.4 us: on_device(): loss = lax.psum(local_loss, 'dp')]
    all_gather x0 -> x4, blocking collectives: none -> 78.7 us  [gather(): return lax.all_gather(value, 'dp', axis=0, tiled=True)]
    ppermute x176 -> x31, waiting for transfers between devices: 160 us -> 122 us  [the longest x15 66.9 us: swap(): return lax.ppermute(value, 'mp', [(0, 1), (1, 0)])]
  transfers between devices with their start and end apart: 191 -> 32, of which waited for: 131 -> 12; matrix products, arithmetic and copies ran while one was open for 5% -> 54% of each run, Pallas kernels for 0% -> 0%
where the time goes in v1:
time: 586 us; the launch traced here: 576 us
  local copies, waits for them, and re-layouts  139 us (24%)
  waiting for transfers between devices  122 us (21%)
  matrix products  104 us (18%)
  other arithmetic  91.3 us (16%)
  blocking collectives  78.7 us (13%)
  starting transfers between devices  20.5 us (3%)
  between operations  20.3 us (3%)
    all_gather x4, blocking collectives, gather(): return lax.all_gather(value, 'dp', axis=0, tiled=True)  78.7 us
    ppermute x15, waiting for transfers between devices, swap(): return lax.ppermute(value, 'mp', [(0, 1), (1, 0)])  66.9 us
    ppermute x16, waiting for transfers between devices, flip(): return lax.ppermute(value, 'dp', [(i, i ^ bit) for i in range(size)])  55.5 us
    dot_general x13, matrix products, dot(): return jnp.dot(a, b, preferred_element_type=F32)  36.5 us
    unnamed x263, local copies, waits for them, and re-layouts  22.3 us
    another operation x12, local copies, waits for them, and re-layouts, attn_backward(): jnp.stack([query_grad, key_grad, value_grad])  20.1 us
    ppermute x15, starting transfers between devices, swap(): return lax.ppermute(value, 'mp', [(0, 1), (1, 0)])  18.5 us
    convert_element_type x12, other arithmetic, halve(): return (keep.astype(F32) + got.astype(F32)).astype(dtype)  12.2 us
  transfers between devices with their start and end apart: 32, of which 12 were waited for; matrix products, arithmetic and copies ran while one was open for 54% of the time, Pallas kernels for 0%

profile of v1, /device:TPU:0, one launch (start us, length us, event | category | flops | bytes accessed | tf_op | source)
XLA Modules:
  0.0 576.0 jit_solution(3225606396276877112)
XLA Ops:
  7.3 3.0 collective-permute-start.1
  19.3 3.0 constant_dynamic-update-slice_fusion.1
  27.6 3.6 dynamic-slice_convert_fusion.1
  31.2 21.8 %all-gather.2 = bf16[16,1,512]{2,1,0:T(2,128)(2,1)S(1)} all-gather(bf16[1,1,512]{2,1,0:T(2,128)(2,1)S(1)} %bitcast.377), channel_id=1, replica_groups=mesh['dp'=16,'mp'=2] {'dp'}, dimensions={0}, use_global_device_ids=true | all-gather | bytes 17408 | tf_op jit(solution)/shard_map/all_gather | solution.py:192
  56.2 17.3 %all-gather.3 = s32[16,1,2]{2,1,0:T(1,128)S(1)} all-gather(s32[1,1,2]{2,1,0:T(1,128)S(1)} %add_bitcast_fusion.3), channel_id=1, replica_groups=mesh['dp'=16,'mp'=2] {'dp'}, dimensions={0}, use_global_device_ids=true | all-gather | bytes 136 | tf_op jit(solution)/shard_map/all_gather | solution.py:192
  74.1 3.6 dynamic-slice_convert_fusion
  79.6 3.5 concatenate.69
  83.2 3.5 fusion.131
  89.2 2.6 multiply_reduce_fusion.7
  92.1 3.2 fusion.26
  103.4 3.5 convert_bitcast_fusion.2
  111.8 3.0 copy.147
  114.8 4.0 fusion
  118.8 2.8 exponential_reduce_fusion
  125.2 3.0 fusion.53
  133.6 2.5 copy.197
  136.2 3.2 gather_fusion.2
  139.4 5.2 copy.223
  144.6 5.4 reshape.689
  150.0 2.5 slice_bitcast_fusion.11
  152.5 3.4 constant_dynamic-update-slice_fusion.2
  156.0 10.1 %multiply_convert_fusion.2 = (bf16[832,3072]{1,0:T(8,128)(2,1)S(1)}, f32[832,3072]{1,0:T(8,128)}) fusion(bf16[832,768]{1,0:T(8,128)(2,1)S(1)} %bitcast.356, bf16[768,3072]{1,0:T(8,128)(2,1)} %constant_dynamic-update-slice_fusion.2), kind=kOutput, calls=%fused_computation.7 | convolution fusion | flops 3941203968 | bytes 21331968 | tf_op jit(solution)/shard_map/dot_general | solution.py:86
  167.9 4.1 fusion.138
  174.7 2.7 slice_bitcast_fusion.1
  180.3 19.7 %all-gather.1 = bf16[16,1,768]{2,1,0:T(2,128)(2,1)S(1)} all-gather(bf16[1,1,768]{2,1,0:T(2,128)(2,1)S(1)} %convert_bitcast_fusion.5), channel_id=1, replica_groups=mesh['dp'=16,'mp'=2] {'dp'}, dimensions={0}, use_global_device_ids=true | all-gather | bytes 26112 | tf_op jit(solution)/shard_map/all_gather | solution.py:192
  205.0 9.9 %multiply_convert_fusion.1 = bf16[832,3072]{1,0:T(8,128)(2,1)S(1)} fusion(f32[832,3072]{1,0:T(8,128)} %get-tuple-element.160, bf16[832,768]{1,0:T(8,128)(2,1)S(1)} %bitcast.352, bf16[3072,768]{1,0:T(8,128)(2,1)S(1)} %constant_dynamic-update-slice_fusion.4), kind=kOutput, calls=%fused_computation.6 | convolution fusion | flops 3951427584 | bytes 21331968 | tf_op jit(solution)/shard_map/dot_general | solution.py:86
  215.0 4.3 multiply_reduce_fusion.5
  219.4 3.7 multiply_reduce_fusion.2
  227.1 6.0 %fusion.129 = (bf16[4,208,768]{2,0,1:T(4,128)(2,1)S(1)}, f32[4,208,768]{2,0,1:T(4,128)}) fusion(f32[4,208]{0,1:T(8,128)} %broadcast_multiply_fusion.2, f32[4,208,768]{2,0,1:T(4,128)} %copy-done.5, f32[4,208]{0,1:T(8,128)S(1)} %broadcast_multiply_fusion.3, f32[4,208]{0,1:T(8,128)} %copy.157, f32[768]{0:T(1024)} %param.37, f32[4,208,768]{2,1,0:T(8,128)} %bitcast.339, ...), kind=kLoop, calls=%fused_computation.306 | loop fusion | flops 5750784 | bytes 11517952 | tf_op jit(solution)/shard_map/convert_element_type | solution.py:265
  234.2 3.5 convolution_convert_fusion.3
  237.7 2.9 copy.159
  240.7 8.0 %convolution_convert_fusion.1 = bf16[4,12,64,208]{3,2,1,0:T(8,128)(2,1)} fusion(bf16[4,208,12,64]{1,3,2,0:T(8,128)(2,1)} %bitcast.342, f32[4,12,208,208]{2,3,1,0:T(8,128)} %copy-done.1, f32[4,12,208]{2,1,0:T(8,128)S(1)} %copy-done.54, pred[208]{0:T(512)(128)(4,1)S(1)} %copy-done.84), kind=kOutput, calls=%fused_computation.80 | convolution fusion | flops 274759680 | bytes 10902736 | tf_op jit(solution)/shard_map/bhqk,bqhe->bkhe/dot_general | solution.py:119
  248.7 9.1 %multiply_reduce_fusion = (f32[4,12,208]{2,1,0:T(8,128)S(1)}, f32[4,12,208,208]{2,3,1,0:T(8,128)S(1)}) fusion(f32[4,12,208,208]{2,3,1,0:T(8,128)} %copy-done.1, f32[4,12,208]{2,1,0:T(8,128)S(1)} %copy-done.54, pred[208]{0:T(512)(128)(4,1)S(1)} %copy-done.84, bf16[4,208,12,64]{1,3,2,0:T(8,128)(2,1)} %bitcast.343, bf16[4,208,12,64]{1,3,2,0:T(8,128)(2,1)} %bitcast.340), kind=kOutput, calls=%fused_computation.5 | convolution fusion | flops 276187392 | bytes 19249360 | tf_op jit(solution)/shard_map/bqhe,bkhe->bhqk/dot_general | solution.py:118
  257.8 3.4 multiply_convert_fusion
  261.2 2.9 multiply_convert_fusion.3
  267.0 2.6 slice_bitcast_fusion.3
  276.4 6.5 %fusion.34 = f32[4,208,768]{2,1,0:T(8,128)S(1)} fusion(bf16[3,768,768]{2,1,0:T(8,128)(2,1)} %copy-done.48, bf16[1,4,208,768]{3,2,0,1:T(8,128)(2,1)} %copy.165, bf16[1,4,208,768]{3,2,0,1:T(8,128)(2,1)} %copy.164, bf16[1,4,208,768]{3,2,0,1:T(8,128)(2,1)} %copy.163), kind=kOutput, calls=%fused_computation.79 | convolution fusion | flops 2948235264 | bytes 9928704 | tf_op jit(solution)/shard_map/kbse,kde->bsd/dot_general | solution.py:126
  283.0 3.7 multiply_reduce_fusion.1
  286.7 2.8 add_bitcast_fusion
  296.1 4.2 stack.105
  300.3 3.8 copy.182
  304.1 4.2 stack.104
  310.7 4.5 stack.103
  327.0 3.4 broadcast_select_fusion
  330.8 4.1 fusion.20
  341.1 5.3 convert_bitcast_fusion.1
  346.4 5.3 convert_bitcast_fusion
  351.7 3.3 fusion.110
  377.8 28.9 %collective-permute-done.17 = bf16[384,384]{0,1:T(8,128)(2,1)} collective-permute-done((bf16[384,384]{0,1:T(8,128)(2,1)S(1)}, bf16[384,384]{0,1:T(8,128)(2,1)}, u32[]{:S(2)}, u32[]{:S(2)}) %collective-permute-start.17) | collective-permute-done | bytes 294944 | tf_op jit(solution)/shard_map/ppermute | solution.py:14
  408.6 19.9 %all-gather.4 = f32[16,3,768]{2,1,0:T(4,128)S(1)} all-gather(f32[1,3,768]{2,1,0:T(4,128)S(1)} %maximum_bitcast_fusion.4), channel_id=2, replica_groups=mesh['dp'=16,'mp'=2] {'dp'}, dimensions={0}, use_global_device_ids=true | all-gather | bytes 156672 | tf_op jit(solution)/shard_map/all_gather | solution.py:192
  429.8 5.0 collective-permute-done.19
  435.5 6.7 %collective-permute-done.20 = bf16[48,384]{0,1:T(8,128)(2,1)S(1)} collective-permute-done((bf16[48,384]{0,1:T(8,128)(2,1)S(1)}, bf16[48,384]{0,1:T(8,128)(2,1)S(1)}, u32[]{:S(2)}, u32[]{:S(2)}) %collective-permute-start.20) | collective-permute-done | bytes 36896 | tf_op jit(solution)/shard_map/ppermute | solution.py:19
  442.9 3.1 broadcast_select_fusion.7
  446.0 2.6 pad_maximum_fusion
  450.9 2.7 pad_maximum_fusion.1
  467.3 3.0 add_convert_fusion.1
  473.3 6.0 %collective-permute-done.12 = bf16[384,1152]{1,0:T(8,128)(2,1)} collective-permute-done((bf16[384,1152]{1,0:T(8,128)(2,1)}, bf16[384,1152]{1,0:T(8,128)(2,1)}, u32[]{:S(2)}, u32[]{:S(2)}) %collective-permute-start.12) | collective-permute-done | bytes 884768 | tf_op jit(solution)/shard_map/ppermute | solution.py:14
  482.4 9.8 %collective-permute-done.13 = bf16[192,1152]{1,0:T(8,128)(2,1)S(1)} collective-permute-done((bf16[192,1152]{1,0:T(8,128)(2,1)S(1)}, bf16[192,1152]{1,0:T(8,128)(2,1)S(1)}, u32[]{:S(2)}, u32[]{:S(2)}) %collective-permute-start.13) | collective-permute-done | bytes 442400 | tf_op jit(solution)/shard_map/ppermute | solution.py:19
  494.2 4.1 collective-permute-done.14
  498.5 6.0 %collective-permute-done.22 = bf16[384,1536]{1,0:T(8,128)(2,1)S(1)} collective-permute-done((bf16[384,1536]{1,0:T(8,128)(2,1)S(1)}, bf16[384,1536]{1,0:T(8,128)(2,1)S(1)}, u32[]{:S(2)}, u32[]{:S(2)}) %collective-permute-start.22) | collective-permute-done | bytes 1179680 | tf_op jit(solution)/shard_map/ppermute | solution.py:14
  505.6 23.7 %collective-permute-done.27 = bf16[384,1536]{1,0:T(8,128)(2,1)S(1)} collective-permute-done((bf16[384,1536]{1,0:T(8,128)(2,1)S(1)}, bf16[384,1536]{1,0:T(8,128)(2,1)S(1)}, u32[]{:S(2)}, u32[]{:S(2)}) %collective-permute-start.27) | collective-permute-done | bytes 1179680 | tf_op jit(solution)/shard_map/ppermute | solution.py:14
  533.7 13.1 %collective-permute-done.28 = bf16[192,1536]{1,0:T(8,128)(2,1)} collective-permute-done((bf16[192,1536]{1,0:T(8,128)(2,1)}, bf16[192,1536]{1,0:T(8,128)(2,1)}, u32[]{:S(2)}, u32[]{:S(2)}) %collective-permute-start.28) | collective-permute-done | bytes 589856 | tf_op jit(solution)/shard_map/ppermute | solution.py:19
  549.1 9.9 %collective-permute-done.29 = bf16[96,1536]{1,0:T(8,128)(2,1)S(1)} collective-permute-done((bf16[96,1536]{1,0:T(8,128)(2,1)S(1)}, bf16[96,1536]{1,0:T(8,128)(2,1)S(1)}, u32[]{:S(2)}, u32[]{:S(2)}) %collective-permute-start.29) | collective-permute-done | bytes 294944 | tf_op jit(solution)/shard_map/ppermute | solution.py:19
  559.9 6.9 %collective-permute-done.30 = bf16[48,1536]{1,0:T(8,128)(2,1)S(1)} collective-permute-done((bf16[48,1536]{1,0:T(8,128)(2,1)S(1)}, bf16[48,1536]{1,0:T(8,128)(2,1)S(1)}, u32[]{:S(2)}, u32[]{:S(2)}) %collective-permute-start.30) | collective-permute-done | bytes 147488 | tf_op jit(solution)/shard_map/ppermute | solution.py:19
  (499 shorter events, 156.9 us)
Async XLA Ops:
  7.2 450.8 %all-gather.7.cloned.1.call-start = ((), (), s32[]{:S(2)}) async-start(), calls=%async_computation | async-start | bytes 1253376 | tf_op jit(solution)/shard_map/all_gather | solution.py:192
  7.3 93.9 %collective-permute-start.1 = (bf16[3,768,384]{2,1,0:T(8,128)(2,1)}, bf16[3,768,384]{2,1,0:T(8,128)(2,1)}, u32[]{:S(2)}, u32[]{:S(2)}) collective-permute-start(bf16[3,768,384]{2,1,0:T(8,128)(2,1)} %param.35), channel_id=1, source_target_pairs={{0,1},{1,0},{2,3},{3,2},{4,5},{5,4},{6,7},{7,6},{8,9},{9,8},{10,11... | collective-permute-start | bytes 5308424 | tf_op jit(solution)/shard_map/ppermute | solution.py:14
  12.0 71.2 %copy-start.45 = (f32[8,768]{1,0:T(8,128)}, f32[8,768]{1,0:T(8,128)S(1)}, u32[]{:S(2)}) copy-start(f32[8,768]{1,0:T(8,128)S(1)} %get-tuple-element.154) | copy-start | bytes 73732
  13.6 10.2 %copy-start.58 = (bf16[8,6,64]{2,1,0:T(8,128)(2,1)}, bf16[8,6,64]{2,1,0:T(8,128)(2,1)S(1)}, u32[]{:S(2)}) copy-start(bf16[8,6,64]{2,1,0:T(8,128)(2,1)S(1)} %reshape.585) | copy-start | bytes 18436
  15.0 8.8 %copy-start.74 = (bf16[8,384]{1,0:T(8,128)(2,1)}, bf16[8,384]{1,0:T(8,128)(2,1)S(1)}, u32[]{:S(2)}) copy-start(bf16[8,384]{1,0:T(8,128)(2,1)S(1)} %convert_element_type.358) | copy-start | bytes 18436
  15.2 68.0 %collective-permute-start = (f32[1,8,768]{2,1,0:T(8,128)S(1)}, f32[1,8,768]{2,1,0:T(8,128)S(1)}, u32[]{:S(2)}, u32[]{:S(2)}) collective-permute-start(f32[1,8,768]{2,1,0:T(8,128)S(1)} %convolution_bitcast_fusion), channel_id=1, source_target_pairs={{0,1},{1,0},{2,3},{3,2},{4,5},{5,4},{6,7},{7,6},{8,9},{9,8},{10,11... | collective-permute-start | bytes 73736 | tf_op jit(solution)/shard_map/ppermute | solution.py:14
  15.4 109.8 %collective-permute-start.2 = (bf16[384,768]{1,0:T(8,128)(2,1)}, bf16[384,768]{1,0:T(8,128)(2,1)}, u32[]{:S(2)}, u32[]{:S(2)}) collective-permute-start(bf16[384,768]{1,0:T(8,128)(2,1)} %param.36), channel_id=1, source_target_pairs={{0,1},{1,0},{2,3},{3,2},{4,5},{5,4},{6,7},{7,6},{8,9},{9,8},{10,11... | collective-permute-start | bytes 1769480 | tf_op jit(solution)/shard_map/ppermute | solution.py:14
  17.2 135.3 %collective-permute-start.3 = (bf16[768,1536]{1,0:T(8,128)(2,1)}, bf16[768,1536]{1,0:T(8,128)(2,1)}, u32[]{:S(2)}, u32[]{:S(2)}) collective-permute-start(bf16[768,1536]{1,0:T(8,128)(2,1)} %param.38), channel_id=1, source_target_pairs={{0,1},{1,0},{2,3},{3,2},{4,5},{5,4},{6,7},{7,6},{8,9},{9,8},{10,11... | collective-permute-start | bytes 7077896 | tf_op jit(solution)/shard_map/ppermute | solution.py:14
  17.4 148.7 %collective-permute-start.4 = (bf16[1536,768]{1,0:T(8,128)(2,1)}, bf16[1536,768]{1,0:T(8,128)(2,1)}, u32[]{:S(2)}, u32[]{:S(2)}) collective-permute-start(bf16[1536,768]{1,0:T(8,128)(2,1)} %param.39), channel_id=1, source_target_pairs={{0,1},{1,0},{2,3},{3,2},{4,5},{5,4},{6,7},{7,6},{8,9},{9,8},{10,11... | collective-permute-start | bytes 7077896 | tf_op jit(solution)/shard_map/ppermute | solution.py:14
  31.2 46.5 %copy-start.113 = (s32[16]{0:T(128)S(1)}, s32[16]{0:T(128)}, u32[]{:S(2)}) copy-start(s32[16]{0:T(128)} %constant.130.clone) | copy-start | bytes 196
  78.3 18.7 %copy-start.89 = (s32[1024]{0:T(1024)}, s32[1024]{0:T(1024)S(1)}, u32[]{:S(2)}) copy-start(s32[1024]{0:T(1024)S(1)} %pad_clamp_fusion) | copy-start | bytes 12292
  78.3 43.4 %copy-start.83 = (pred[208]{0:T(512)(128)(4,1)}, pred[208]{0:T(512)(128)(4,1)S(1)}, u32[]{:S(2)}) copy-start(pred[208]{0:T(512)(128)(4,1)S(1)} %iota_compare_fusion) | copy-start | bytes 628
  89.1 9.7 %copy-start.27 = (f32[4,208]{0,1:T(8,128)}, f32[4,208]{0,1:T(8,128)S(1)}, u32[]{:S(2)}) copy-start(f32[4,208]{0,1:T(8,128)S(1)} %broadcast_multiply_fusion.4) | copy-start | bytes 9988
  152.5 13.5 %slice-start.7 = ((s8[4718592]{0:T(1024)(128)(4,1)}), s8[4194304]{0:T(1024)(128)(4,1)S(1)}, s32[]{:S(2)}) async-start(s8[4718592]{0:T(1024)(128)(4,1)} %bitcast.368), calls=%async_computation.8 | async-start | bytes 8388608
  156.0 10.1 %slice-start.8 = ((s8[4718592]{0:T(1024)(128)(4,1)}), s8[524288]{0:T(1024)(128)(4,1)S(1)}, s32[]{:S(2)}) async-start(s8[4718592]{0:T(1024)(128)(4,1)} %bitcast.368), calls=%async_computation.9 | async-start | bytes 1048576
  174.0 6.2 %collective-permute-start.6 = (f32[1,768]{1,0:T(1,128)S(1)}, f32[1,768]{1,0:T(1,128)S(1)}, u32[]{:S(2)}, u32[]{:S(2)}) collective-permute-start(f32[1,768]{1,0:T(1,128)S(1)} %reduce_sum.290), channel_id=1, source_target_pairs={{0,1},{1,0},{2,3},{3,2},{4,5},{5,4},{6,7},{7,6},{8,9},{9,8},{10,11... | collective-permute-start | bytes 9224 | tf_op jit(solution)/shard_map/ppermute | solution.py:14
  174.7 25.3 %copy-start.31 = (bf16[768,512]{1,0:T(8,128)(2,1)S(1)}, bf16[768,512]{1,0:T(8,128)(2,1)}, u32[]{:S(2)}) copy-start(bf16[768,512]{1,0:T(8,128)(2,1)} %param.40) | copy-start | bytes 2359300
  177.4 22.9 %copy-start.70 = (bf16[16,1,512]{2,0,1:T(8,128)(2,1)S(1)}, bf16[16,1,512]{2,0,1:T(8,128)(2,1)}, u32[]{:S(2)}) copy-start(bf16[16,1,512]{2,0,1:T(8,128)(2,1)} %copy-done.69) | copy-start | bytes 49156
  177.4 22.9 %copy-start.112 = (f32[16]{0:T(128)S(1)}, f32[16]{0:T(128)}, u32[]{:S(2)}) copy-start(f32[16]{0:T(128)} %get-tuple-element.149) | copy-start | bytes 196
  177.4 23.7 %copy-start.96 = (s32[16]{0:T(128)S(1)}, s32[16]{0:T(128)}, u32[]{:S(2)}) copy-start(s32[16]{0:T(128)} %get-tuple-element.141) | copy-start | bytes 196
  177.4 23.7 %copy-start.98 = (s32[16]{0:T(128)S(1)}, s32[16]{0:T(128)}, u32[]{:S(2)}) copy-start(s32[16]{0:T(128)} %get-tuple-element.142) | copy-start | bytes 196
  177.4 25.5 %copy-start.7 = (f32[1,4,208,768]{3,1,2,0:T(4,128)S(1)}, f32[1,4,208,768]{3,1,2,0:T(4,128)}, u32[]{:S(2)}) copy-start(f32[1,4,208,768]{3,1,2,0:T(4,128)} %concatenate.69) | copy-start | bytes 7667716
  178.9 264.1 %collective-permute-start.5 = (bf16[1,4,197,768]{3,1,2,0:T(4,128)(2,1)}, bf16[1,4,197,768]{3,1,2,0:T(4,128)(2,1)}, u32[]{:S(2)}, u32[]{:S(2)}) collective-permute-start(bf16[1,4,197,768]{3,1,2,0:T(4,128)(2,1)} %slice.470), channel_id=1, source_target_pairs={{0,1},{1,0},{2,3},{3,2},{4,5},{5,4},{6,7},{7,6},{8,9},{9,8},{10,11... | collective-permute-start | bytes 3631112 | tf_op jit(solution)/shard_map/ppermute | solution.py:14
  204.1 10.8 %slice-start.9 = ((s8[4718592]{0:T(1024)(128)(4,1)}), s8[4194304]{0:T(1024)(128)(4,1)S(1)}, s32[]{:S(2)}) async-start(s8[4718592]{0:T(1024)(128)(4,1)} %bitcast.370), calls=%async_computation.10 | async-start | bytes 8388608
  205.0 9.9 %copy-start.18 = (bf16[1,4,208,768]{3,2,1,0:T(8,128)(2,1)}, bf16[1,4,208,768]{3,2,1,0:T(8,128)(2,1)S(1)}, u32[]{:S(2)}) copy-start(bf16[1,4,208,768]{3,2,1,0:T(8,128)(2,1)S(1)} %copy.155) | copy-start | bytes 3833860
  205.0 9.9 %slice-start.10 = ((s8[4718592]{0:T(1024)(128)(4,1)}), s8[524288]{0:T(1024)(128)(4,1)S(1)}, s32[]{:S(2)}) async-start(s8[4718592]{0:T(1024)(128)(4,1)} %bitcast.370), calls=%async_computation.11 | async-start | bytes 1048576
  205.0 10.0 %copy-start.81 = (f32[768]{0:T(1024)S(1)}, f32[768]{0:T(1024)}, u32[]{:S(2)}) copy-start(f32[768]{0:T(1024)} %param.37) | copy-start | bytes 9220
  240.6 17.2 %slice-start = ((s8[10223616]{0:T(1024)(128)(4,1)}), s8[4194304]{0:T(1024)(128)(4,1)S(1)}, s32[]{:S(2)}) async-start(s8[10223616]{0:T(1024)(128)(4,1)} %bitcast.328), calls=%async_computation.1 | async-start | bytes 8388608
  240.6 17.2 %slice-start.1 = ((s8[10223616]{0:T(1024)(128)(4,1)}), s8[4194304]{0:T(1024)(128)(4,1)S(1)}, s32[]{:S(2)}) async-start(s8[10223616]{0:T(1024)(128)(4,1)} %bitcast.328), calls=%async_computation.2 | async-start | bytes 8388608
  248.7 9.1 %slice-start.2 = ((s8[10223616]{0:T(1024)(128)(4,1)}), s8[1835008]{0:T(1024)(128)(4,1)S(1)}, s32[]{:S(2)}) async-start(s8[10223616]{0:T(1024)(128)(4,1)} %bitcast.328), calls=%async_computation.3 | async-start | bytes 3670016
  291.1 71.1 %collective-permute-start.7 = (f32[1,4,768]{2,1,0:T(4,128)S(1)}, f32[1,4,768]{2,1,0:T(4,128)S(1)}, u32[]{:S(2)}, u32[]{:S(2)}) collective-permute-start(f32[1,4,768]{2,1,0:T(4,128)S(1)} %slice_bitcast_fusion.14), channel_id=1, source_target_pairs={{0,1},{1,0},{2,3},{3,2},{4,5},{5,4},{6,7},{7,6},{8,9},{9,8},{10,11... | collective-permute-start | bytes 36872 | tf_op jit(solution)/shard_map/ppermute | solution.py:14
  293.1 68.5 %collective-permute-start.10 = (f32[2,768]{1,0:T(2,128)S(1)}, f32[2,768]{1,0:T(2,128)S(1)}, u32[]{:S(2)}, u32[]{:S(2)}) collective-permute-start(f32[2,768]{1,0:T(2,128)S(1)} %pad_maximum_fusion.5), channel_id=1, source_target_pairs={{0,1},{1,0},{2,3},{3,2},{4,5},{5,4},{6,7},{7,6},{8,9},{9,8},{10,11... | collective-permute-start | bytes 18440 | tf_op jit(solution)/shard_map/ppermute | solution.py:14
  336.3 117.3 %collective-permute-start.11 = (bf16[2,384,1152]{2,1,0:T(8,128)(2,1)}, bf16[2,384,1152]{2,1,0:T(8,128)(2,1)}, u32[]{:S(2)}, u32[]{:S(2)}) collective-permute-start(bf16[2,384,1152]{2,1,0:T(8,128)(2,1)} %slice.358), channel_id=1, source_target_pairs={{0,2},{2,0},{4,6},{6,4},{8,10},{10,8},{12,14},{14,12},{16,18},{18,... | collective-permute-start | bytes 5308424 | tf_op jit(solution)/shard_map/ppermute | solution.py:19
  338.6 7.8 %copy-start.43 = (bf16[2,768,384]{1,2,0:T(8,128)(2,1)}, bf16[2,768,384]{1,2,0:T(8,128)(2,1)S(1)}, u32[]{:S(2)}) copy-start(bf16[2,768,384]{1,2,0:T(8,128)(2,1)S(1)} %fusion.39) | copy-start | bytes 3538948
  339.5 34.9 %collective-permute-start.16 = (bf16[2,384,384]{1,2,0:T(8,128)(2,1)}, bf16[2,384,384]{1,2,0:T(8,128)(2,1)}, u32[]{:S(2)}, u32[]{:S(2)}) collective-permute-start(bf16[2,384,384]{1,2,0:T(8,128)(2,1)} %slice.370), channel_id=1, source_target_pairs={{0,2},{2,0},{4,6},{6,4},{8,10},{10,8},{12,14},{14,12},{16,18},{18,... | collective-permute-start | bytes 1769480 | tf_op jit(solution)/shard_map/ppermute | solution.py:19
  346.4 10.7 %copy-start.25 = (bf16[2,768,1536]{2,1,0:T(8,128)(2,1)}, bf16[2,768,1536]{2,1,0:T(8,128)(2,1)S(1)}, u32[]{:S(2)}) copy-start(bf16[2,768,1536]{2,1,0:T(8,128)(2,1)S(1)} %convert_bitcast_fusion.1) | copy-start | bytes 14155780
  360.2 9.7 %copy-start.46 = (f32[8,768]{1,0:T(8,128)S(1)}, f32[8,768]{1,0:T(8,128)}, u32[]{:S(2)}) copy-start(f32[8,768]{1,0:T(8,128)} %copy-done.45) | copy-start | bytes 73732
  360.2 9.7 %copy-start.68 = (f32[768]{0:T(1024)S(1)}, f32[768]{0:T(1024)}, u32[]{:S(2)}) copy-start(f32[768]{0:T(1024)} %param.31) | copy-start | bytes 9220
  360.2 9.7 %copy-start.86 = (f32[8]{0:T(128)S(1)}, f32[8]{0:T(128)}, u32[]{:S(2)}) copy-start(f32[8]{0:T(128)} %copy-done.85) | copy-start | bytes 100
  360.2 9.7 %copy-start.88 = (f32[8]{0:T(128)S(1)}, f32[8]{0:T(128)}, u32[]{:S(2)}) copy-start(f32[8]{0:T(128)} %copy-done.87) | copy-start | bytes 100
  360.2 10.0 %copy-start.60 = (bf16[8,4608]{1,0:T(8,128)(2,1)S(1)}, bf16[8,4608]{1,0:T(8,128)(2,1)}, u32[]{:S(2)}) copy-start(bf16[8,4608]{1,0:T(8,128)(2,1)} %constant_dynamic-update-slice_fusion.11) | copy-start | bytes 221188
  361.6 105.7 %collective-permute-start.21 = (bf16[2,384,1536]{2,1,0:T(8,128)(2,1)}, bf16[2,384,1536]{2,1,0:T(8,128)(2,1)}, u32[]{:S(2)}, u32[]{:S(2)}) collective-permute-start(bf16[2,384,1536]{2,1,0:T(8,128)(2,1)} %slice.382), channel_id=1, source_target_pairs={{0,2},{2,0},{4,6},{6,4},{8,10},{10,8},{12,14},{14,12},{16,18},{18,... | collective-permute-start | bytes 7077896 | tf_op jit(solution)/shard_map/ppermute | solution.py:19
  365.5 8.8 %copy-start.44 = (bf16[2,768,384]{1,2,0:T(8,128)(2,1)S(1)}, bf16[2,768,384]{1,2,0:T(8,128)(2,1)}, u32[]{:S(2)}) copy-start(bf16[2,768,384]{1,2,0:T(8,128)(2,1)} %copy-done.43) | copy-start | bytes 3538948
  365.5 11.5 %copy-start.75 = (bf16[8,384]{1,0:T(8,128)(2,1)S(1)}, bf16[8,384]{1,0:T(8,128)(2,1)}, u32[]{:S(2)}) copy-start(bf16[8,384]{1,0:T(8,128)(2,1)} %copy-done.74) | copy-start | bytes 18436
  366.1 3.9 collective-permute-start.8
  372.8 75.8 %collective-permute-start.9 = (bf16[1,4,197,768]{3,1,2,0:T(4,128)(2,1)S(1)}, bf16[1,4,197,768]{3,1,2,0:T(4,128)(2,1)}, u32[]{:S(2)}, u32[]{:S(2)}) collective-permute-start(bf16[1,4,197,768]{3,1,2,0:T(4,128)(2,1)S(1)} %fusion.77), channel_id=1, source_target_pairs={{0,1},{1,0},{2,3},{3,2},{4,5},{5,4},{6,7},{7,6},{8,9},{9,8},{10,11... | collective-permute-start | bytes 3631112 | tf_op jit(solution)/shard_map/ppermute | solution.py:14
  376.4 30.2 %collective-permute-start.17 = (bf16[384,384]{0,1:T(8,128)(2,1)S(1)}, bf16[384,384]{0,1:T(8,128)(2,1)}, u32[]{:S(2)}, u32[]{:S(2)}) collective-permute-start(bf16[384,384]{0,1:T(8,128)(2,1)S(1)} %slice_bitcast_fusion.12), channel_id=1, source_target_pairs={{0,1},{1,0},{2,3},{3,2},{4,5},{5,4},{6,7},{7,6},{8,9},{9,8},{10,11... | collective-permute-start | bytes 884744 | tf_op jit(solution)/shard_map/ppermute | solution.py:14
  408.6 20.0 %collective-permute-start.18 = (bf16[192,384]{0,1:T(8,128)(2,1)}, bf16[192,384]{0,1:T(8,128)(2,1)}, u32[]{:S(2)}, u32[]{:S(2)}) collective-permute-start(bf16[192,384]{0,1:T(8,128)(2,1)} %slice.374), channel_id=1, source_target_pairs={{0,4},{2,6},{4,0},{6,2},{8,12},{10,14},{12,8},{14,10},{16,20},{18,... | collective-permute-start | bytes 442376 | tf_op jit(solution)/shard_map/ppermute | solution.py:19
  429.6 5.1 collective-permute-start.19
  434.9 7.3 %collective-permute-start.20 = (bf16[48,384]{0,1:T(8,128)(2,1)S(1)}, bf16[48,384]{0,1:T(8,128)(2,1)S(1)}, u32[]{:S(2)}, u32[]{:S(2)}) collective-permute-start(bf16[48,384]{0,1:T(8,128)(2,1)S(1)} %slice.378), channel_id=1, source_target_pairs={{0,16},{2,18},{4,20},{6,22},{8,24},{10,26},{12,28},{14,30},{16,0},... | collective-permute-start | bytes 110600 | tf_op jit(solution)/shard_map/ppermute | solution.py:19
  442.1 28.9 %collective-permute-start.26 = (bf16[2,384,1536]{2,1,0:T(8,128)(2,1)}, bf16[2,384,1536]{2,1,0:T(8,128)(2,1)}, u32[]{:S(2)}, u32[]{:S(2)}) collective-permute-start(bf16[2,384,1536]{2,1,0:T(8,128)(2,1)} %slice.394), channel_id=1, source_target_pairs={{0,2},{2,0},{4,6},{6,4},{8,10},{10,8},{12,14},{14,12},{16,18},{18,... | collective-permute-start | bytes 7077896 | tf_op jit(solution)/shard_map/ppermute | solution.py:19
  456.5 22.8 %collective-permute-start.12 = (bf16[384,1152]{1,0:T(8,128)(2,1)}, bf16[384,1152]{1,0:T(8,128)(2,1)}, u32[]{:S(2)}, u32[]{:S(2)}) collective-permute-start(bf16[384,1152]{1,0:T(8,128)(2,1)} %slice_bitcast_fusion.8), channel_id=1, source_target_pairs={{0,1},{1,0},{2,3},{3,2},{4,5},{5,4},{6,7},{7,6},{8,9},{9,8},{10,11... | collective-permute-start | bytes 2654216 | tf_op jit(solution)/shard_map/ppermute | solution.py:14
  470.4 34.1 %collective-permute-start.22 = (bf16[384,1536]{1,0:T(8,128)(2,1)S(1)}, bf16[384,1536]{1,0:T(8,128)(2,1)S(1)}, u32[]{:S(2)}, u32[]{:S(2)}) collective-permute-start(bf16[384,1536]{1,0:T(8,128)(2,1)S(1)} %slice_bitcast_fusion.6), channel_id=1, source_target_pairs={{0,1},{1,0},{2,3},{3,2},{4,5},{5,4},{6,7},{7,6},{8,9},{9,8},{10,11... | collective-permute-start | bytes 3538952 | tf_op jit(solution)/shard_map/ppermute | solution.py:14
  480.7 11.5 %collective-permute-start.13 = (bf16[192,1152]{1,0:T(8,128)(2,1)S(1)}, bf16[192,1152]{1,0:T(8,128)(2,1)S(1)}, u32[]{:S(2)}, u32[]{:S(2)}) collective-permute-start(bf16[192,1152]{1,0:T(8,128)(2,1)S(1)} %slice.362), channel_id=1, source_target_pairs={{0,4},{2,6},{4,0},{6,2},{8,12},{10,14},{12,8},{14,10},{16,20},{18,... | collective-permute-start | bytes 1327112 | tf_op jit(solution)/shard_map/ppermute | solution.py:19
  480.9 48.5 %collective-permute-start.27 = (bf16[384,1536]{1,0:T(8,128)(2,1)S(1)}, bf16[384,1536]{1,0:T(8,128)(2,1)S(1)}, u32[]{:S(2)}, u32[]{:S(2)}) collective-permute-start(bf16[384,1536]{1,0:T(8,128)(2,1)S(1)} %slice_bitcast_fusion.4), channel_id=1, source_target_pairs={{0,1},{1,0},{2,3},{3,2},{4,5},{5,4},{6,7},{7,6},{8,9},{9,8},{10,11... | collective-permute-start | bytes 3538952 | tf_op jit(solution)/shard_map/ppermute | solution.py:14
  492.3 6.0 %collective-permute-start.14 = (bf16[96,1152]{1,0:T(8,128)(2,1)S(1)}, bf16[96,1152]{1,0:T(8,128)(2,1)S(1)}, u32[]{:S(2)}, u32[]{:S(2)}) collective-permute-start(bf16[96,1152]{1,0:T(8,128)(2,1)S(1)} %slice.364), channel_id=1, source_target_pairs={{0,8},{2,10},{4,12},{6,14},{8,0},{10,2},{12,4},{14,6},{16,24},{18,... | collective-permute-start | bytes 663560 | tf_op jit(solution)/shard_map/ppermute | solution.py:19
  498.4 33.1 %collective-permute-start.15 = (bf16[48,1152]{1,0:T(8,128)(2,1)S(1)}, bf16[48,1152]{1,0:T(8,128)(2,1)S(1)}, u32[]{:S(2)}, u32[]{:S(2)}) collective-permute-start(bf16[48,1152]{1,0:T(8,128)(2,1)S(1)} %slice.366), channel_id=1, source_target_pairs={{0,16},{2,18},{4,20},{6,22},{8,24},{10,26},{12,28},{14,30},{16,0},... | collective-permute-start | bytes 331784 | tf_op jit(solution)/shard_map/ppermute | solution.py:19
  505.6 26.7 %collective-permute-start.23 = (bf16[192,1536]{1,0:T(8,128)(2,1)}, bf16[192,1536]{1,0:T(8,128)(2,1)}, u32[]{:S(2)}, u32[]{:S(2)}) collective-permute-start(bf16[192,1536]{1,0:T(8,128)(2,1)} %slice.386), channel_id=1, source_target_pairs={{0,4},{2,6},{4,0},{6,2},{8,12},{10,14},{12,8},{14,10},{16,20},{18,... | collective-permute-start | bytes 1769480 | tf_op jit(solution)/shard_map/ppermute | solution.py:19
  531.5 15.3 %collective-permute-start.28 = (bf16[192,1536]{1,0:T(8,128)(2,1)}, bf16[192,1536]{1,0:T(8,128)(2,1)}, u32[]{:S(2)}, u32[]{:S(2)}) collective-permute-start(bf16[192,1536]{1,0:T(8,128)(2,1)} %slice.398), channel_id=1, source_target_pairs={{0,4},{2,6},{4,0},{6,2},{8,12},{10,14},{12,8},{14,10},{16,20},{18,... | collective-permute-start | bytes 1769480 | tf_op jit(solution)/shard_map/ppermute | solution.py:19
  531.6 15.1 %copy-start.23 = (bf16[384,1536]{1,0:T(8,128)(2,1)S(1)}, bf16[384,1536]{1,0:T(8,128)(2,1)}, u32[]{:S(2)}) copy-start(bf16[384,1536]{1,0:T(8,128)(2,1)} %copy-done.22) | copy-start | bytes 3538948
  533.6 14.5 %collective-permute-start.24 = (bf16[96,1536]{1,0:T(8,128)(2,1)S(1)}, bf16[96,1536]{1,0:T(8,128)(2,1)S(1)}, u32[]{:S(2)}, u32[]{:S(2)}) collective-permute-start(bf16[96,1536]{1,0:T(8,128)(2,1)S(1)} %slice.388), channel_id=1, source_target_pairs={{0,8},{2,10},{4,12},{6,14},{8,0},{10,2},{12,4},{14,6},{16,24},{18,... | collective-permute-start | bytes 884744 | tf_op jit(solution)/shard_map/ppermute | solution.py:19
  548.0 11.0 %collective-permute-start.29 = (bf16[96,1536]{1,0:T(8,128)(2,1)S(1)}, bf16[96,1536]{1,0:T(8,128)(2,1)S(1)}, u32[]{:S(2)}, u32[]{:S(2)}) collective-permute-start(bf16[96,1536]{1,0:T(8,128)(2,1)S(1)} %slice.400), channel_id=1, source_target_pairs={{0,8},{2,10},{4,12},{6,14},{8,0},{10,2},{12,4},{14,6},{16,24},{18,... | collective-permute-start | bytes 884744 | tf_op jit(solution)/shard_map/ppermute | solution.py:19
  548.2 11.0 %collective-permute-start.25 = (bf16[48,1536]{1,0:T(8,128)(2,1)S(1)}, bf16[48,1536]{1,0:T(8,128)(2,1)S(1)}, u32[]{:S(2)}, u32[]{:S(2)}) collective-permute-start(bf16[48,1536]{1,0:T(8,128)(2,1)S(1)} %slice.390), channel_id=1, source_target_pairs={{0,16},{2,18},{4,20},{6,22},{8,24},{10,26},{12,28},{14,30},{16,0},... | collective-permute-start | bytes 442376 | tf_op jit(solution)/shard_map/ppermute | solution.py:19
  559.1 7.7 %collective-permute-start.30 = (bf16[48,1536]{1,0:T(8,128)(2,1)S(1)}, bf16[48,1536]{1,0:T(8,128)(2,1)S(1)}, u32[]{:S(2)}, u32[]{:S(2)}) collective-permute-start(bf16[48,1536]{1,0:T(8,128)(2,1)S(1)} %slice.402), channel_id=1, source_target_pairs={{0,16},{2,18},{4,20},{6,22},{8,24},{10,26},{12,28},{14,30},{16,0},... | collective-permute-start | bytes 442376 | tf_op jit(solution)/shard_map/ppermute | solution.py:19
  (95 other events, 304.1 us)
Sparse Core Ops, SparseCore 0:
  377.9 35.5 all-gather.6
